TPU v7x, 128 devices: a whole 4x4x4 slice. The times are simulated.
128 devices in a mesh: grp: 8 (over y, core), dev: 16 (over x, z).
Axes of the slice: x: 4, y: 4, z: 4, core: 2. Of those that a mesh axis runs over, the one named last changes fastest.
Arguments:
- latent: bfloat16 [8192, 128, 512], P('grp', 'dev'), may hold values from -6 to 6
- value_up: bfloat16 [128, 512, 128], P('dev'), may hold values from -0.25 to 0.25
- out_proj: bfloat16 [16384, 7168], P('dev'), may hold values from -0.0625 to 0.0625
- adapter_down: bfloat16 [32, 256, 16384], P('grp', None, 'dev'), may hold values from -0.046875 to 0.046875
- adapter_up: bfloat16 [32, 256, 7168], P('grp', None, 'dev'), may hold values from -0.375 to 0.375
- pair_ids: int32 [32, 2], P('grp'), may hold values from 0 to 31, as said below
- mix_weights: float32 [2, 8192], P(None, 'grp'), may hold values from 0.25 to 1
Outputs:
- projected: bfloat16 [8192, 7168], P('grp', 'dev')
Inputs may be any that keep to these rules, and one draw needn't show every extreme that they name: `pair_ids`: adapter a belongs to index a // 4 of grp. Among the 8 adapter picks of the blocks of one index of grp, at most 2 name adapters of one index of grp, and in every index of grp some index of grp receives exactly 2. The two adapters of a block differ.
All inputs are finite; a program needn't handle non-finite values.
Results may differ from a plain program's by a relative error of at most 0.02.
Values may be sent and summed in bfloat16 or wider, within the bound.
A program may use at most 192 MiB of HBM per device.

v0:
```python
import jax
import jax.numpy as jnp
from jax import lax
from jax.sharding import PartitionSpec as P

CAP = 2


def local(latent, value_up, out_proj, adapter_down, adapter_up, pair_ids, mix_weights):
    total_rows = latent.shape[0]
    row_block_count = pair_ids.shape[0]
    block_rows = total_rows // row_block_count
    selection_count = 2 * row_block_count
    owned = adapter_down.shape[0]
    head_cols = adapter_down.shape[2]
    col_count = adapter_up.shape[2]
    adapter_groups = lax.axis_size("grp")
    capacity = CAP
    heads_out = jnp.einsum("rhl,hlv->rhv", latent, value_up, preferred_element_type=jnp.float32)
    heads_out = heads_out.astype(jnp.bfloat16).reshape(total_rows, head_cols)
    partial_base = jnp.dot(heads_out, out_proj, preferred_element_type=jnp.float32)
    base_projection = lax.psum_scatter(
        partial_base.astype(jnp.bfloat16), "dev", scatter_dimension=1, tiled=True
    ).astype(jnp.float32)
    x_blocks = heads_out.reshape(row_block_count, block_rows, head_cols)
    flat_ids = pair_ids.reshape(selection_count)
    owner_of = flat_ids // owned
    local_of = flat_ids % owned
    order = jnp.arange(selection_count, dtype=jnp.int32)
    earlier = (owner_of[:, None] == owner_of[None, :]) & (order[None, :] < order[:, None])
    position = jnp.sum(earlier.astype(jnp.int32), axis=1)
    slot_of = owner_of * capacity + position
    slot_total = adapter_groups * capacity
    hits = jnp.arange(slot_total, dtype=jnp.int32)[:, None] == slot_of[None, :]
    select = hits.astype(jnp.bfloat16)
    slot_local = jnp.sum(hits.astype(jnp.int32) * local_of[None, :], axis=1).reshape(
        adapter_groups, capacity
    )
    select_blocks = jnp.sum(select.reshape(slot_total, row_block_count, 2), axis=2)
    outbound = jnp.einsum(
        "sb,brc->src", select_blocks, x_blocks, preferred_element_type=jnp.float32
    )
    outbound = outbound.astype(jnp.bfloat16).reshape(
        adapter_groups, capacity, block_rows, head_cols
    )
    piece = lax.all_to_all(outbound, "grp", split_axis=0, concat_axis=0, tiled=True)
    local_ids = lax.all_to_all(slot_local, "grp", split_axis=0, concat_axis=0, tiled=True)
    chosen = jnp.take(adapter_down, local_ids, axis=0)
    images = jnp.einsum("gmrc,gmkc->gmrk", piece, chosen, preferred_element_type=jnp.float32)
    low = lax.psum(images.astype(jnp.bfloat16), "dev")
    chosen_up = jnp.take(adapter_up, local_ids, axis=0)
    lifted = jnp.einsum("gmrk,gmkc->gmrc", low, chosen_up, preferred_element_type=jnp.float32)
    lifted = lifted.astype(jnp.bfloat16)
    inbound = lax.all_to_all(lifted, "grp", split_axis=0, concat_axis=0, tiled=True)
    inbound = inbound.reshape(slot_total, block_rows, col_count)
    lifted_picks = jnp.einsum("sp,src->prc", select, inbound, preferred_element_type=jnp.float32)
    weights = jnp.transpose(mix_weights.reshape(2, row_block_count, block_rows), (1, 0, 2))
    lifted_picks = lifted_picks.reshape(row_block_count, 2, block_rows, col_count)
    adapter_term = jnp.sum(lifted_picks * weights[:, :, :, None], axis=1).reshape(
        total_rows, col_count
    )
    return (base_projection + adapter_term).astype(jnp.bfloat16)


def solution(mesh):
    placed = (
        P("grp", "dev", None),
        P("dev", None, None),
        P("dev", None),
        P("grp", None, "dev"),
        P("grp", None, "dev"),
        P("grp", None),
        P(None, "grp"),
    )
    return jax.shard_map(
        local, mesh=mesh, in_specs=placed, out_specs=P("grp", "dev"), check_vma=False
    )
```

profile of v0, /device:TPU:1, one launch (start us, length us, event | category | flops | bytes accessed | tf_op | source)
XLA Modules:
  0.0 376.5 jit_solution(8290033351957937708)
XLA Ops:
  6.5 0.0 copy-start
  6.5 0.9 copy.58
  7.5 0.1 reshape.184
  7.6 0.2 convert_reduce_fusion
  7.7 0.1 select_reduce_fusion
  7.8 0.7 all_to_all.17
  8.5 6.0 %all-to-all-start.1 = ((s32[8,1,2]{2,1,0:T(1,128)}), s32[8,1,2]{2,1,0:T(1,128)S(1)}, u32[]{:S(2)}, u32[]{:S(2)}) async-start(s32[8,1,2]{2,1,0:T(1,128)} %bitcast.4), calls=%async_computation.2 | async-start | bytes 8192 | tf_op jit(solution)/shard_map/all_to_all | solution.py:47
  14.5 0.1 reduce_sum.42
  14.6 0.1 copy.63
  14.7 0.1 fusion.33
  14.8 10.3 %fusion.23 = bf16[8,128,1024]{2,1,0:T(8,128)(2,1)} fusion(bf16[8,512,128]{2,1,0:T(8,128)(2,1)} %param.8, bf16[1024,8,512]{2,1,0:T(8,128)(2,1)} %param.7), kind=kOutput, calls=%fused_computation.20 | convolution fusion | flops 1074790400 | bytes 11534336 | tf_op jit(solution)/shard_map/rhl,hlv->rhv/dot_general | solution.py:19
  25.1 4.5 %reshape_reshape.3 = bf16[4,256,1024]{1,0,2:T(4,128)(2,1)} reshape(bf16[1024,8,128]{0,2,1:T(8,128)(2,1)} %bitcast.39) | data formatting | bytes 4194304 | tf_op jit(solution)/shard_map/reshape;reshape | solution.py:25
  29.6 5.7 %copy.64 = bf16[4,256,1024]{2,0,1:T(4,128)(2,1)} copy(bf16[4,256,1024]{1,0,2:T(4,128)(2,1)} %reshape_reshape.3) | data formatting | bytes 4194304 | tf_op jit(solution)/shard_map/reshape;reshape | solution.py:25
  35.3 6.0 %convolution_convert_fusion.1 = bf16[16,256,1024]{2,0,1:T(8,128)(2,1)} fusion(bf16[4,256,1024]{2,0,1:T(4,128)(2,1)} %copy.64, bf16[16,4]{0,1:T(4,128)(2,1)S(1)} %fusion.33), kind=kOutput, calls=%fused_computation.9 | convolution fusion | flops 37748736 | bytes 10485888 | tf_op jit(solution)/shard_map/sb,brc->src/dot_general | solution.py:40
  41.2 13.1 %reshape.185 = bf16[8,2,256,1024]{3,1,0,2:T(2,128)(2,1)} reshape(bf16[16,256,1024]{2,0,1:T(8,128)(2,1)} %convolution_convert_fusion.1) | data formatting | bytes 16777216 | tf_op jit(solution)/shard_map/reshape | solution.py:43
  54.3 8.1 %copy.65 = bf16[8,2,256,1024]{3,1,2,0:T(2,128)(2,1)} copy(bf16[8,2,256,1024]{3,1,0,2:T(2,128)(2,1)} %reshape.185) | data formatting | bytes 16777216 | tf_op jit(solution)/shard_map/reshape | solution.py:43
  62.4 0.0 all-to-all-done.1
  62.4 5.0 %all-to-all-start = ((bf16[8,2,256,1024]{3,1,2,0:T(2,128)(2,1)}), bf16[8,2,256,1024]{3,1,2,0:T(2,128)(2,1)}, u32[]{:S(2)}, u32[]{:S(2)}) async-start(bf16[8,2,256,1024]{3,1,2,0:T(2,128)(2,1)} %copy.65), calls=%async_computation.1 | async-start | bytes 16777216 | tf_op jit(solution)/shard_map/all_to_all | solution.py:46
  67.4 0.0 all-reduce.2.cloned.1.call-start
  67.4 0.1 copy.67
  67.5 0.1 copy.68
  67.6 0.1 copy.70
  67.7 0.1 reshape.191
  67.8 0.0 copy-done
  67.8 4.5 %gather_fusion = bf16[16,256,1024]{2,1,0:T(8,128)(2,1)} fusion(bf16[4,256,1024]{2,1,0:T(8,128)(2,1)S(1)} %copy-done, s32[1024]{0:T(1024)S(1)} %pad_clamp_fusion), kind=kCustom, calls=%fused_computation | custom fusion | bytes 16777280 | tf_op jit(solution)/shard_map/jit(_take)/gather | solution.py:48
  72.4 88.8 %all-to-all-done = bf16[8,2,256,1024]{3,1,2,0:T(2,128)(2,1)} async-done(((bf16[8,2,256,1024]{3,1,2,0:T(2,128)(2,1)}), bf16[8,2,256,1024]{3,1,2,0:T(2,128)(2,1)}, u32[]{:S(2)}, u32[]{:S(2)}) %all-to-all-start) | async-done | bytes 8388640 | tf_op jit(solution)/shard_map/all_to_all | solution.py:46
  161.2 0.0 copy-start.3
  161.2 9.8 %fusion.18 = bf16[8,2,256,256]{3,2,1,0:T(8,128)(2,1)} fusion(bf16[8,2,256,1024]{3,2,1,0:T(8,128)(2,1)} %bitcast.36, pred[8,2]{1,0:T(8,128)(4,1)S(1)} %copy.68, bf16[8,2,256,1024]{3,1,2,0:T(2,128)(2,1)} %all-to-all-done), kind=kOutput, calls=%fused_computation.19 | convolution fusion | flops 2152726528 | bytes 18874384 | tf_op jit(solution)/shard_map/gmrc,gmkc->gmrk/dot_general | solution.py:49
  171.0 0.0 all-reduce.2.cloned.1.call-update
  171.0 0.2 reduce-scatter.2.cloned.1.call-start
  171.3 0.0 copy-done.3
  171.3 31.3 %convolution_convert_fusion = bf16[1024,7168]{0,1:T(8,128)(2,1)} fusion(bf16[1024,1024]{0,1:T(8,128)(2,1)S(1)} %bitcast.40, bf16[1024,7168]{1,0:T(8,128)(2,1)} %param.9), kind=kOutput, calls=%fused_computation.2 | convolution fusion | flops 15039725568 | bytes 31457280 | tf_op jit(solution)/shard_map/dot_general | solution.py:21
  202.6 0.0 copy-start.2
  202.6 0.0 reduce-scatter.2.cloned.1.call-update
  202.6 1.2 copy-done.2
  203.8 2.6 gather_fusion.1
  206.4 54.6 %all-reduce.2.cloned.1.call-done = bf16[8,2,256,256]{3,2,1,0:T(8,128)(2,1)} async-done(((bf16[8,2,256,256]{3,2,1,0:T(8,128)(2,1)}), bf16[8,2,256,256]{3,2,1,0:T(8,128)(2,1)}) %all-reduce.2.cloned.1.call-update) | async-done | bytes 2097168 | tf_op jit(solution)/shard_map/psum | solution.py:50
  261.0 5.7 %fusion.13 = bf16[8,2,256,448]{2,3,1,0:T(8,128)(2,1)} fusion(bf16[8,2,256,256]{3,2,1,0:T(8,128)(2,1)} %all-reduce.2.cloned.1.call-done, bf16[8,2,256,448]{2,3,1,0:T(8,128)(2,1)} %bitcast.38, pred[8,2]{1,0:T(8,128)(4,1)S(1)} %copy.68), kind=kOutput, calls=%fused_computation.18 | convolution fusion | flops 943194112 | bytes 9437200 | tf_op jit(solution)/shard_map/gmrk,gmkc->gmrc/dot_general | solution.py:52
  266.7 6.2 %all-to-all-start.2 = ((bf16[8,2,256,448]{2,3,1,0:T(8,128)(2,1)}), bf16[8,2,256,448]{2,3,1,0:T(8,128)(2,1)}, u32[]{:S(2)}, u32[]{:S(2)}) async-start(bf16[8,2,256,448]{2,3,1,0:T(8,128)(2,1)} %fusion.13), calls=%async_computation.3 | async-start | bytes 7340032 | tf_op jit(solution)/shard_map/all_to_all | solution.py:54
  272.9 0.1 iota_compare_fusion.3
  273.0 0.0 copy-done.4
  273.0 43.2 %all-to-all-done.2 = bf16[8,2,256,448]{2,3,1,0:T(8,128)(2,1)} async-done(((bf16[8,2,256,448]{2,3,1,0:T(8,128)(2,1)}), bf16[8,2,256,448]{2,3,1,0:T(8,128)(2,1)}, u32[]{:S(2)}, u32[]{:S(2)}) %all-to-all-start.2) | async-done | bytes 3670048 | tf_op jit(solution)/shard_map/all_to_all | solution.py:54
  316.2 5.3 %multiply_reduce_fusion = f32[4,256,448]{1,0,2:T(4,128)S(1)} fusion(bf16[16,256,448]{1,2,0:T(8,128)(2,1)} %bitcast.9, f32[4,2,256]{2,0,1:T(4,128)S(1)} %bitcast.42, pred[4,2,16,1]{2,1,0,3:T(4,128)(4,1)S(1)} %bitcast.43), kind=kOutput, calls=%fused_computation.14 | convolution fusion | flops 30736384 | bytes 5513344 | tf_op jit(solution)/shard_map/sp,src->prc/dot_general | solution.py:56
  321.6 0.0 copy-start.1
  321.6 1.6 copy.79
  323.2 43.4 %reduce-scatter.2.cloned.1.call-done = bf16[1024,448]{0,1:T(8,128)(2,1)} async-done(((bf16[1024,7168]{0,1:T(8,128)(2,1)}), bf16[1024,448]{0,1:T(8,128)(2,1)}) %reduce-scatter.2.cloned.1.call-update) | async-done | bytes 917520 | tf_op jit(solution)/shard_map/reduce_scatter | solution.py:22
  366.7 3.0 add_convert_fusion
  369.6 0.0 copy-done.1
  (9 shorter events, 0.1 us)
Async XLA Ops:
  6.5 61.3 %copy-start = (bf16[4,256,1024]{2,1,0:T(8,128)(2,1)S(1)}, bf16[4,256,1024]{2,1,0:T(8,128)(2,1)}, u32[]{:S(2)}) copy-start(bf16[4,256,1024]{2,1,0:T(8,128)(2,1)} %param.10) | copy-start | bytes 6291460
  8.5 53.9 %all-to-all-start.1 = ((s32[8,1,2]{2,1,0:T(1,128)}), s32[8,1,2]{2,1,0:T(1,128)S(1)}, u32[]{:S(2)}, u32[]{:S(2)}) async-start(s32[8,1,2]{2,1,0:T(1,128)} %bitcast.4), calls=%async_computation.2 | async-start | bytes 8192 | tf_op jit(solution)/shard_map/all_to_all | solution.py:47
  62.4 98.8 %all-to-all-start = ((bf16[8,2,256,1024]{3,1,2,0:T(2,128)(2,1)}), bf16[8,2,256,1024]{3,1,2,0:T(2,128)(2,1)}, u32[]{:S(2)}, u32[]{:S(2)}) async-start(bf16[8,2,256,1024]{3,1,2,0:T(2,128)(2,1)} %copy.65), calls=%async_computation.1 | async-start | bytes 16777216 | tf_op jit(solution)/shard_map/all_to_all | solution.py:46
  67.4 193.6 %all-reduce.2.cloned.1.call-start = ((), (), s32[]{:S(2)}) async-start(), calls=%async_computation.5 | async-start | bytes 4194304 | tf_op jit(solution)/shard_map/psum | solution.py:50
  161.2 10.1 %copy-start.3 = (bf16[8,128,1024]{2,1,0:T(8,128)(2,1)S(1)}, bf16[8,128,1024]{2,1,0:T(8,128)(2,1)}, u32[]{:S(2)}) copy-start(bf16[8,128,1024]{2,1,0:T(8,128)(2,1)} %fusion.23) | copy-start | bytes 6291460
  171.0 195.6 %reduce-scatter.2.cloned.1.call-start = ((), (), s32[]{:S(2)}) async-start(), calls=%async_computation.4 | async-start | bytes 15597568 | tf_op jit(solution)/shard_map/reduce_scatter | solution.py:22
  202.6 1.2 copy-start.2
  266.7 6.3 %copy-start.4 = (f32[2,1024]{1,0:T(2,128)S(1)}, f32[2,1024]{1,0:T(2,128)}, u32[]{:S(2)}) copy-start(f32[2,1024]{1,0:T(2,128)} %param.13) | copy-start | bytes 24580
  266.7 49.6 %all-to-all-start.2 = ((bf16[8,2,256,448]{2,3,1,0:T(8,128)(2,1)}), bf16[8,2,256,448]{2,3,1,0:T(8,128)(2,1)}, u32[]{:S(2)}, u32[]{:S(2)}) async-start(bf16[8,2,256,448]{2,3,1,0:T(8,128)(2,1)} %fusion.13), calls=%async_computation.3 | async-start | bytes 7340032 | tf_op jit(solution)/shard_map/all_to_all | solution.py:54
  321.6 48.0 %copy-start.1 = (bf16[4,256,1024]{2,1,0:T(8,128)(2,1)S(1)}, bf16[4,256,1024]{2,1,0:T(8,128)(2,1)}, u32[]{:S(2)}) copy-start(bf16[4,256,1024]{2,1,0:T(8,128)(2,1)} %param.10) | copy-start | bytes 6291460
Sparse Core Ops, SparseCore 0:
  171.2 89.7 all-reduce.1
  264.8 101.8 reduce-scatter.1
where the time goes:
time: 377 us; the launch traced here: 376 us
  waiting for transfers between devices  230 us (61%)
  matrix products  68.5 us (18%)
  local copies, waits for them, and re-layouts  43.5 us (12%)
  starting transfers between devices  17.4 us (5%)
  between operations  13.5 us (4%)
    all_to_all x1, waiting for transfers between devices, local(): lax.all_to_all(outbound, 'grp', split_axis=0, concat_axis=0, tiled=True)  88.8 us
    psum x1, waiting for transfers between devices, local(): low = lax.psum(images.astype(jnp.bfloat16), 'dev')  54.6 us
    reduce_scatter x1, waiting for transfers between devices, local(): lax.psum_scatter(partial_base.astype(jnp.bfloat16), 'dev', scatter_dimens...  43.4 us
    all_to_all x1, waiting for transfers between devices, local(): lax.all_to_all(lifted, 'grp', split_axis=0, concat_axis=0, tiled=True)  43.2 us
    dot_general x1, matrix products, local(): jnp.dot(heads_out, out_proj, preferred_element_type=jnp.float32)  31.3 us
    reshape x2, local copies, waits for them, and re-layouts, local(): outbound.astype(jnp.bfloat16)  21.2 us
    dot_general x1, matrix products, local(): jnp.einsum('rhl,hlv->rhv', latent, value_up, preferred_element_type=jnp.f...  10.3 us
    another operation x2, local copies, waits for them, and re-layouts, local(): x_blocks = heads_out.reshape(row_block_count, block_rows, head_cols)  10.2 us
  transfers between devices with their start and end apart: 5, of which 4 were waited for; matrix products, arithmetic and copies ran while one was open for 26% of the time, Pallas kernels for 0%

commit v1 on v0

v1 whole, which is shorter than its diff:
```python
import functools

import jax
import jax.numpy as jnp
from jax import lax
from jax.experimental import pallas as pl
from jax.experimental.pallas import tpu as pltpu
from jax.sharding import PartitionSpec as P

MESH = pl.DeviceIdType.MESH
F32 = jnp.float32
BF16 = jnp.bfloat16
CHUNKS = 7
LAG = 4
P_SLOTS = 3
S1_SLOTS = 3
S23_SLOTS = 5
R_SLOTS = 3


def roll64(x):
    return pltpu.roll(x, 64, 1)


def kernel(
    latent, value_up, out_proj, down, up_t, ids, mix, out,
    wide, vup, heads, w, p, s1r, s2r, s3r, r, t1r, t2r, t3r, f,
    gdn, gup, low, l1r, mid, l2r, lowf,
    lat_sem, vup_sem, w_sem, own_sem,
    s_send, s_recv, t_send, t_recv, y_send, y_recv, l_send, l_recv,
):
    g = lax.axis_index("grp")
    d = lax.axis_index("dev")
    y, core = g // 2, g % 2
    x, z = d // 4, d % 4

    def at(yy=None, cc=None, xx=None, zz=None):
        yy = y if yy is None else yy
        cc = core if cc is None else cc
        xx = x if xx is None else xx
        zz = z if zz is None else zz
        return (yy * 2 + cc, xx * 4 + zz)

    def off(v, k):
        return lax.rem(v + k, 4)

    y_up, y_down, sibling = at(yy=off(y, 1)), at(yy=off(y, 3)), at(cc=1 - core)
    x_at = [None] + [at(xx=off(x, k)) for k in (1, 2, 3)]
    z_at = [None] + [at(zz=off(z, k)) for k in (1, 2, 3)]

    def remote(src, dst, send, recv, to):
        return pltpu.make_async_remote_copy(
            src_ref=src, dst_ref=dst, send_sem=send, recv_sem=recv, device_id=to, device_id_type=MESH
        )

    barrier = pltpu.get_barrier_semaphore()
    for n in x_at[1:] + z_at[1:] + [y_up, y_down, sibling]:
        pl.semaphore_signal(barrier, inc=1, device_id=n, device_id_type=MESH)

    def lat_start(c, slot):
        for k in range(4):
            for m in range(4):
                pltpu.make_async_copy(
                    latent.at[pl.ds(pl.multiple_of(c * 2048 + m * 512, 512), 512), pl.ds(k * 128, 128)],
                    p.at[slot, k, m], lat_sem.at[slot]).start()

    def lat_wait(slot):
        pltpu.make_async_copy(p.at[slot], p.at[slot], lat_sem.at[slot]).wait()

    def w_start(t, slot):
        @pl.loop(0, 8)
        def _(q):
            for par in range(2):
                pltpu.make_async_copy(
                    out_proj.at[:, pl.ds(pl.multiple_of(q * 896 + par * 512 + t * 128, 128), 128)],
                    w.at[slot, q, :, pl.ds(par * 128, 128)], w_sem.at[slot]).start()

    def w_start_tail(slot):
        @pl.loop(0, 8)
        def _(q):
            pltpu.make_async_copy(
                out_proj.at[:, pl.ds(pl.multiple_of(q * 896 + 384, 128), 128)],
                w.at[slot, q, :, pl.ds(0, 128)], w_sem.at[slot]).start()

    def w_wait(slot):
        pltpu.make_async_copy(w.at[slot], w.at[slot], w_sem.at[slot]).wait()

    vup_copy = pltpu.make_async_copy(value_up, vup, vup_sem)
    vup_copy.start()
    lat_start(0, 0)
    lat_start(1, 1)
    pl.semaphore_wait(barrier, 9)

    own = g * 4

    def block(yy, cc):
        return (yy * 2 + cc) * 4

    def adapters(kind, src, gathered):
        base = kind * 16
        below, above, across = block(off(y, 3), core), block(off(y, 1), core), block(off(y, 2), core)

        def cp(k, source, unit, count, to):
            return remote(source, gathered.at[pl.ds(unit, count)], y_send.at[base + k], y_recv.at[base + k], to)

        def here(unit, count):
            return gathered.at[pl.ds(unit, count)]

        first = [
            cp(0, src.at[pl.ds(0, 2)], own, 2, y_up),
            cp(1, src.at[pl.ds(2, 2)], own + 2, 2, y_down),
            cp(2, src.at[pl.ds(2, 2)], own + 2, 2, y_up),
            cp(3, src.at[pl.ds(0, 2)], own, 2, y_down),
            cp(4, src, own, 4, sibling),
        ]
        second = [
            cp(5, here(below, 2), below, 2, y_up),
            cp(6, here(above + 2, 2), above + 2, 2, y_down),
            cp(7, here(below, 4), below, 4, sibling),
            cp(8, here(above, 4), above, 4, sibling),
        ]
        third = [
            cp(9, here(across, 2), across, 2, sibling),
            cp(10, here(across + 2, 2), across + 2, 2, sibling),
        ]
        return first, second, third

    dn1, dn2, dn3 = adapters(0, down, gdn)
    up1, up2, up3 = adapters(1, up_t, gup)

    def start(copies):
        for c in copies:
            c.start()

    def got(copies):
        for c in copies:
            c.wait_recv()

    start(dn1)
    own_dn = pltpu.make_async_copy(down, gdn.at[pl.ds(own, 4)], own_sem.at[0])
    own_up = pltpu.make_async_copy(up_t, gup.at[pl.ds(own, 4)], own_sem.at[1])
    own_dn.start()
    own_up.start()
    w_start(0, 0)
    w_start(1, 1)

    vup_copy.wait()

    @pl.loop(0, 4)
    def _(c):
        slot = lax.rem(c, 2)
        lat_wait(slot)
        for k in range(4):
            for m in range(4):
                wide[k, pl.ds(m * 512, 512), :] = p[slot, k, m].astype(F32)

        @pl.when(c < 2)
        def _():
            lat_start(c + 2, slot)

        for h in range(8):
            xh = jnp.concatenate([wide[k, pl.ds(h, 256, stride=8), :] for k in range(4)], axis=1).astype(BF16)
            heads[pl.ds(pl.multiple_of(c * 256, 256), 256), pl.ds(h * 128, 128)] = jnp.dot(
                xh, vup[h], preferred_element_type=F32).astype(BF16)

    coord = (x, z)
    ring = (x_at, z_at)

    def piece(slot, dim, dest, half):
        rows = pl.ds(dim * 256 + half * 128, 128)
        return p.at[slot, dest, :, rows, :] if dim == 0 else p.at[slot, :, dest, rows, :]

    def s_copies(c, kind):
        slot, n1, n5 = lax.rem(c, P_SLOTS), lax.rem(c, S1_SLOTS), lax.rem(c, S23_SLOTS)
        copies = []
        for dim in range(2):
            me, to = coord[dim], ring[dim]
            plus, opp, minus = off(me, 1), off(me, 2), off(me, 3)
            what = {0: ((opp, 0), (opp, 1)), 1: ((plus, 1), (minus, 0)), 2: ((plus, 0), (minus, 1))}[kind]
            land = (s1r.at[n1], s2r.at[n5], s3r.at[n5])[kind]
            for way in range(2):
                dest, half = what[way]
                copies.append(remote(
                    piece(slot, dim, dest, half), land.at[dim, way],
                    s_send.at[kind, c, dim, way], s_recv.at[kind, c, dim, way], to[1] if way == 0 else to[3]))
        return copies

    def t_copies(c, kind):
        slot = lax.rem(c, R_SLOTS)
        copies = []
        for dim in range(2):
            me, to = coord[1 - dim], ring[1 - dim]
            plus, opp, minus = off(me, 1), off(me, 2), off(me, 3)
            what = {0: ((opp, 0), (opp, 1)), 1: ((plus, 1), (minus, 0)), 2: ((plus, 0), (minus, 1))}[kind]
            land = (t1r, t2r, t3r)[kind]
            for way in range(2):
                dest, half = what[way]
                copies.append(remote(
                    r.at[slot, dim, dest, pl.ds(half * 128, 128), :], land.at[c, dim, way],
                    t_send.at[kind, c, dim, way], t_recv.at[kind, c, dim, way], to[1] if way == 0 else to[3]))
        return copies

    def produce(c):
        slot = lax.rem(c, P_SLOTS)

        @pl.when(c >= P_SLOTS)
        def _():
            for kind in range(3):
                for cp in s_copies(c - P_SLOTS, kind):
                    cp.wait_send()

        @pl.when(c < 6)
        def _():
            wslot = lax.rem(c // 2, 2)

            @pl.when(lax.rem(c, 2) == 0)
            def _():
                w_wait(wslot)

            rows = pl.ds(pl.multiple_of(lax.rem(c, 2) * 512, 512), 512)

            @pl.loop(0, 8)
            def _(q):
                o = jnp.dot(heads[rows, :], w[wslot, q], preferred_element_type=F32).astype(BF16)
                p[slot, q // 2, lax.rem(q, 2) * 2] = o[:, :128]
                p[slot, q // 2, lax.rem(q, 2) * 2 + 1] = o[:, 128:]

            @pl.when(c == 1)
            def _():
                w_start(2, 0)

            @pl.when(c == 3)
            def _():
                w_start_tail(1)

        @pl.when(c == 6)
        def _():
            tail = w.at[1, :, :, pl.ds(0, 128)]
            pltpu.make_async_copy(tail, tail, w_sem.at[1]).wait()
            lane = lax.broadcasted_iota(jnp.int32, (512, 128), 1)

            @pl.loop(0, 8)
            def _(q):
                wq = w[1, q, :, pl.ds(0, 128)]
                top = jnp.dot(heads[pl.ds(0, 512), :], wq, preferred_element_type=F32)
                bottom = jnp.dot(heads[pl.ds(512, 512), :], wq, preferred_element_type=F32)
                p[slot, q // 2, lax.rem(q, 2) * 2] = jnp.where(lane < 64, top, roll64(bottom)).astype(BF16)
                p[slot, q // 2, lax.rem(q, 2) * 2 + 1] = jnp.where(lane < 64, roll64(top), bottom).astype(BF16)

        start(s_copies(c, 0))
        start(s_copies(c, 1))

    def pass_on(c):
        slot, n1 = lax.rem(c, P_SLOTS), lax.rem(c, S1_SLOTS)
        got(s_copies(c, 0))
        for dim in range(2):
            for way in range(2):
                dest = off(coord[dim], 1 if way == 0 else 3)
                ref = piece(slot, dim, dest, way)
                ref[...] = (ref[...].astype(F32) + s1r[n1, dim, way].astype(F32)).astype(BF16)
        start(s_copies(c, 2))

    def reduce_first(c):
        slot, n5, rs = lax.rem(c, P_SLOTS), lax.rem(c, S23_SLOTS), lax.rem(c, R_SLOTS)
        got(s_copies(c, 1))
        got(s_copies(c, 2))
        for dim in range(2):
            for half in range(2):
                mine = piece(slot, dim, coord[dim], half)[...].astype(F32)
                total = mine + s3r[n5, dim, half].astype(F32) + s2r[n5, dim, 1 - half].astype(F32)
                r[rs, dim, :, pl.ds(half * 128, 128), :] = total.astype(BF16)
        start(t_copies(c, 0))
        start(t_copies(c, 1))

    def pass_on_second(c):
        rs = lax.rem(c, R_SLOTS)
        got(t_copies(c, 0))
        for dim in range(2):
            for way in range(2):
                dest = off(coord[1 - dim], 1 if way == 0 else 3)
                ref = r.at[rs, dim, dest, pl.ds(way * 128, 128), :]
                ref[...] = (ref[...].astype(F32) + t1r[c, dim, way].astype(F32)).astype(BF16)
        start(t_copies(c, 2))

    def reduce_second(c):
        rs = lax.rem(c, R_SLOTS)
        got(t_copies(c, 1))
        got(t_copies(c, 2))
        for dim in range(2):
            for half in range(2):
                mine = r[rs, dim, coord[1 - dim], pl.ds(half * 128, 128), :].astype(F32)
                f[c, pl.ds(dim * 256 + half * 128, 128), :] = (
                    mine + t3r[c, dim, half].astype(F32) + t2r[c, dim, 1 - half].astype(F32))
        for kind in range(3):
            for cp in t_copies(c, kind):
                cp.wait_send()

    def l_copies(phase):
        copies = []
        for dim in range(2):
            me, to = coord[dim], ring[dim]
            other, to_other = coord[1 - dim], ring[1 - dim]
            mine = dim * 4 + me
            part = pl.ds(pl.multiple_of(other * 64, 64), 64)
            for k in range(1, 4):
                if phase == 0:
                    src, dst, dev = low.at[dim * 4 + off(me, k)], l1r.at[dim, k - 1], to[k]
                elif phase == 1:
                    src = mid.at[dim, pl.ds(pl.multiple_of(off(other, k) * 64, 64), 64), :]
                    dst, dev = l2r.at[dim, k - 1], to_other[k]
                elif phase == 2:
                    src = dst = lowf.at[mine, part, :]
                    dev = to_other[k]
                else:
                    src = dst = lowf.at[mine]
                    dev = to[k]
                copies.append(remote(src, dst, l_send.at[phase, dim, k - 1], l_recv.at[phase, dim, k - 1], dev))
        return copies

    def low_images():
        own_dn.wait()
        got(dn1[4:])
        got(dn2[2:])
        got(dn3)

        @pl.loop(0, 8)
        def _(q):
            rows = pl.ds(pl.multiple_of((q // 2) * 256, 256), 256)
            chosen = gdn[ids[q // 2, lax.rem(q, 2)]]
            low[q] = lax.dot_general(
                heads[rows, :], chosen, (((1,), (1,)), ((), ())), preferred_element_type=F32).astype(BF16)

        start(l_copies(0))

    def low_second():
        got(l_copies(0))
        for dim in range(2):
            total = low[dim * 4 + coord[dim]].astype(F32)
            for k in range(3):
                total = total + l1r[dim, k].astype(F32)
            mid[dim] = total.astype(BF16)
        start(l_copies(1))

    def low_third():
        got(l_copies(1))
        for dim in range(2):
            part = pl.ds(pl.multiple_of(coord[1 - dim] * 64, 64), 64)
            total = mid[dim, part, :].astype(F32)
            for k in range(3):
                total = total + l2r[dim, k].astype(F32)
            lowf[dim * 4 + coord[dim], part, :] = total.astype(BF16)
        start(l_copies(2))

    def low_fourth():
        got(l_copies(2))
        start(l_copies(3))

    @pl.loop(0, CHUNKS + LAG)
    def _(i):
        @pl.when(i < CHUNKS)
        def _():
            produce(i)

        @pl.when((i >= 1) & (i < CHUNKS + 1))
        def _():
            pass_on(i - 1)

        @pl.when((i >= 2) & (i < CHUNKS + 2))
        def _():
            reduce_first(i - 2)

        @pl.when((i >= 3) & (i < CHUNKS + 3))
        def _():
            pass_on_second(i - 3)

        @pl.when(i >= 4)
        def _():
            reduce_second(i - 4)

        @pl.when(i == 4)
        def _():
            got(dn1[:4])
            start(dn2)

        @pl.when(i == 6)
        def _():
            got(dn2[:2])
            start(dn3)
            start(up1)

        @pl.when(i == 7)
        def _():
            low_images()

        @pl.when(i == 8)
        def _():
            low_second()

        @pl.when(i == 9)
        def _():
            low_third()
            got(up1[:4])
            start(up2)

        @pl.when(i == 10)
        def _():
            low_fourth()

    for c in range(CHUNKS - P_SLOTS, CHUNKS):
        for kind in range(3):
            for cp in s_copies(c, kind):
                cp.wait_send()
    got(l_copies(3))
    got(up2[:2])
    start(up3)
    own_up.wait()
    got(up1[4:])
    got(up2[2:])
    got(up3)

    lane = lax.broadcasted_iota(jnp.int32, (256, 128), 1)
    for b in range(4):
        half, at_row = b // 2, (b % 2) * 256
        rows = pl.ds(b * 256, 256)
        lifted = None
        for k in range(2):
            li = lax.dot_general(
                lowf[b * 2 + k], gup[ids[b, k]], (((1,), (1,)), ((), ())),
                preferred_element_type=F32).astype(BF16).astype(F32)
            weight = jnp.broadcast_to(mix[k:k + 1, b * 256:(b + 1) * 256], (128, 256)).T
            li = [li[:, :128] * weight, li[:, 128:256] * weight, li[:, 256:384] * weight, li[:, 384:] * weight[:, :64]]
            lifted = li if lifted is None else [u + v for u, v in zip(lifted, li)]
        main = [f[2 * t + half, pl.ds(at_row, 256), :] for t in range(3)]
        tail = f[6, pl.ds(at_row, 256), :]
        if half == 1:
            tail = roll64(tail)

        def write(tiles):
            for t in range(3):
                out[rows, pl.ds(t * 128, 128)] = (tiles[t] + lifted[t]).astype(BF16)
            out[rows, pl.ds(384, 64)] = (tiles[3][:, :64] + lifted[3]).astype(BF16)

        @pl.when(lax.rem(z, 2) == 0)
        def _():
            write(main + [tail])

        @pl.when(lax.rem(z, 2) == 1)
        def _():
            turned = [roll64(m) for m in main]
            write([
                jnp.where(lane < 64, tail, turned[0]),
                jnp.where(lane < 64, turned[0], turned[1]),
                jnp.where(lane < 64, turned[1], turned[2]),
                turned[2],
            ])

    for copies in (dn1, dn2, dn3, up1, up2, up3, l_copies(0), l_copies(1), l_copies(2), l_copies(3)):
        for cp in copies:
            cp.wait_send()


def local(latent, value_up, out_proj, adapter_down, adapter_up, pair_ids, mix_weights):
    rows = latent.shape[0]
    any_ = pl.BlockSpec(memory_space=pl.ANY)
    vmem = pl.BlockSpec(memory_space=pltpu.VMEM)
    smem = pl.BlockSpec(memory_space=pltpu.SMEM)
    dma = pltpu.SemaphoreType.DMA
    scratch = [
        pltpu.VMEM((4, 2048, 128), F32),
        pltpu.VMEM((8, 512, 128), BF16),
        pltpu.VMEM((rows, 1024), BF16),
        pltpu.VMEM((2, 8, 1024, 256), BF16),
        pltpu.VMEM((P_SLOTS, 4, 4, 512, 128), BF16),
        pltpu.VMEM((S1_SLOTS, 2, 2, 4, 128, 128), BF16),
        pltpu.VMEM((S23_SLOTS, 2, 2, 4, 128, 128), BF16),
        pltpu.VMEM((S23_SLOTS, 2, 2, 4, 128, 128), BF16),
        pltpu.VMEM((R_SLOTS, 2, 4, 256, 128), BF16),
        pltpu.VMEM((CHUNKS, 2, 2, 128, 128), BF16),
        pltpu.VMEM((CHUNKS, 2, 2, 128, 128), BF16),
        pltpu.VMEM((CHUNKS, 2, 2, 128, 128), BF16),
        pltpu.VMEM((CHUNKS, 512, 128), F32),
        pltpu.VMEM((32, 256, 1024), BF16),
        pltpu.VMEM((32, 448, 256), BF16),
        pltpu.VMEM((8, 256, 256), BF16),
        pltpu.VMEM((2, 3, 256, 256), BF16),
        pltpu.VMEM((2, 256, 256), BF16),
        pltpu.VMEM((2, 3, 64, 256), BF16),
        pltpu.VMEM((8, 256, 256), BF16),
        dma((2,)), dma, dma((2,)), dma((2,)),
        dma((3, CHUNKS, 2, 2)), dma((3, CHUNKS, 2, 2)),
        dma((3, CHUNKS, 2, 2)), dma((3, CHUNKS, 2, 2)),
        dma((32,)), dma((32,)),
        dma((4, 2, 3)), dma((4, 2, 3)),
    ]
    return pl.pallas_call(
        kernel,
        out_shape=jax.ShapeDtypeStruct((rows, adapter_up.shape[2]), BF16),
        in_specs=[any_, any_, any_, any_, any_, smem, vmem],
        out_specs=vmem,
        scratch_shapes=scratch,
        compiler_params=pltpu.CompilerParams(
            collective_id=1, has_side_effects=True, vmem_limit_bytes=64 << 20),
        name="project",
    )(
        latent.reshape(rows * 8, 512), value_up, out_proj, adapter_down,
        jnp.swapaxes(adapter_up, 1, 2), pair_ids, mix_weights,
    )


def solution(mesh):
    placed = (
        P("grp", "dev", None),
        P("dev", None, None),
        P("dev", None),
        P("grp", None, "dev"),
        P("grp", None, "dev"),
        P("grp", None),
        P(None, "grp"),
    )
    return jax.shard_map(
        local, mesh=mesh, in_specs=placed, out_specs=P("grp", "dev"), check_vma=False
    )
```

time: 377 us -> 129 us (0.34)
  waiting for transfers between devices: 230 us -> 0 us
  Pallas kernels: 0 us -> 125 us
  matrix products: 68.5 us -> 0 us
  local copies, waits for them, and re-layouts: 43.5 us -> 3.55 us
  starting transfers between devices: 17.4 us -> 0 us
  between operations: 13.5 us -> 0.01 us
    all_to_all x3 -> x0, waiting for transfers between devices: 132 us -> none  [the longest x1 88.8 us: local(): lax.all_to_all(outbound, 'grp', split_axis=0, concat_axis=0, tiled=True)]
    pallas_call x0 -> x1, Pallas kernels: none -> 125 us  [local(): pl.pallas_call(kernel, out_shape=jax.ShapeDtypeStruct((rows, adapter_up.s...]
    dot_general x6 -> x0, matrix products: 68.5 us -> none  [the longest x1 31.3 us: local(): jnp.dot(heads_out, out_proj, preferred_element_type=jnp.float32)]
    psum x1 -> x0, waiting for transfers between devices: 54.6 us -> none  [local(): low = lax.psum(images.astype(jnp.bfloat16), 'dev')]
    reduce_scatter x1 -> x0, waiting for transfers between devices: 43.4 us -> none  [local(): lax.psum_scatter(partial_base.astype(jnp.bfloat16), 'dev', scatter_dimens...]
    reshape x4 -> x0, local copies, waits for them, and re-layouts: 21.3 us -> none  [the longest x2 21.2 us: local(): outbound.astype(jnp.bfloat16)]
    all_to_all x3 -> x0, starting transfers between devices: 17.2 us -> none  [the longest x1 6.24 us: local(): lax.all_to_all(lifted, 'grp', split_axis=0, concat_axis=0, tiled=True)]
    another operation x2 -> x0, local copies, waits for them, and re-layouts: 10.2 us -> none  [local(): x_blocks = heads_out.reshape(row_block_count, block_rows, head_cols)]
  transfers between devices with their start and end apart: 5 -> 0, of which waited for: 4 -> 0; matrix products, arithmetic and copies ran while one was open for 26% -> 0% of each run, Pallas kernels for 0% -> 0%
where the time goes in v1:
time: 129 us; the launch traced here: 128 us
  Pallas kernels  125 us (97%)
  local copies, waits for them, and re-layouts  3.55 us (3%)
    pallas_call x1, Pallas kernels, local(): pl.pallas_call(kernel, out_shape=jax.ShapeDtypeStruct((rows, adapter_up.s...  125 us

profile of v1, /device:TPU:1, one launch (start us, length us, event | category | flops | bytes accessed | tf_op | source)
XLA Modules:
  0.0 128.4 jit_solution(7914934936248787125)
XLA Ops:
  0.0 1.3 %copy.8.ids = s32[4,2]{1,0:T(4,128)} copy(s32[4,2]{0,1:T(2,128)} %param.12) | data formatting | bytes 64 | tf_op args[5]
  1.3 124.8 %project.1 = bf16[1024,448]{1,0:T(8,128)(2,1)} custom-call(bf16[8192,512]{1,0:T(8,128)(2,1)} %bitcast.2, bf16[8,512,128]{2,1,0:T(8,128)(2,1)} %value_up.1, bf16[1024,7168]{1,0:T(8,128)(2,1)} %out_proj.1, bf16[4,256,1024]{2,1,0:T(8,128)(2,1)} %down.1, bf16[4,448,256]{2,1,0:T(8,128)(2,1)} %bitcast.3, s32[4,2]{1,0:T(4,128)} %copy.8.ids, f32[2,1024]{1,0:T(2,128)} %mix.1), custom_call_target="tpu_custom_call" | custom-call | tf_op jit(solution)/shard_map/project/pallas_call | solution.py:495
  126.2 2.2 %copy.9 = bf16[1024,448]{0,1:T(8,128)(2,1)} copy(bf16[1024,448]{1,0:T(8,128)(2,1)} %project.1) | data formatting | bytes 1835008 | tf_op jit(solution)/shard_map/project/pallas_call | solution.py:495

commit v2 on v1

--- a/solution.py
+++ b/solution.py
@@ -24,10 +24,10 @@
 
 def kernel(
     latent, value_up, out_proj, down, up_t, ids, mix, out,
-    wide, vup, heads, w, p, s1r, s2r, s3r, r, t1r, t2r, t3r, f,
-    gdn, gup, low, l1r, mid, l2r, lowf,
-    lat_sem, vup_sem, w_sem, own_sem,
-    s_send, s_recv, t_send, t_recv, y_send, y_recv, l_send, l_recv,
+    wide, vup, heads, w, p, s1r, s23r, r, t1r, t23r, f,
+    gdn, gup, low, l1r, mid, l2r, lowf, staged,
+    lat_sem, vup_sem, w_sem, own_sem, out_sem,
+    s_send, s1_recv, s23_recv, t_send, t1_recv, t23_recv, y_send, y_recv, l_send, l_recv,
 ):
     g = lax.axis_index("grp")
     d = lax.axis_index("dev")
@@ -48,6 +48,9 @@
     x_at = [None] + [at(xx=off(x, k)) for k in (1, 2, 3)]
     z_at = [None] + [at(zz=off(z, k)) for k in (1, 2, 3)]
 
+    def arrived(ref, sem):
+        pltpu.make_async_copy(ref, ref, sem).wait()
+
     def remote(src, dst, send, recv, to):
         return pltpu.make_async_remote_copy(
             src_ref=src, dst_ref=dst, send_sem=send, recv_sem=recv, device_id=to, device_id_type=MESH
@@ -62,10 +65,10 @@
             for m in range(4):
                 pltpu.make_async_copy(
                     latent.at[pl.ds(pl.multiple_of(c * 2048 + m * 512, 512), 512), pl.ds(k * 128, 128)],
-                    p.at[slot, k, m], lat_sem.at[slot]).start()
+                    p.at[slot + 1, k, m], lat_sem.at[slot]).start()
 
     def lat_wait(slot):
-        pltpu.make_async_copy(p.at[slot], p.at[slot], lat_sem.at[slot]).wait()
+        arrived(p.at[slot + 1], lat_sem.at[slot])
 
     def w_start(t, slot):
         @pl.loop(0, 8)
@@ -83,12 +86,13 @@
                 w.at[slot, q, :, pl.ds(0, 128)], w_sem.at[slot]).start()
 
     def w_wait(slot):
-        pltpu.make_async_copy(w.at[slot], w.at[slot], w_sem.at[slot]).wait()
+        arrived(w.at[slot], w_sem.at[slot])
 
     vup_copy = pltpu.make_async_copy(value_up, vup, vup_sem)
     vup_copy.start()
     lat_start(0, 0)
     lat_start(1, 1)
+    w_start(0, 0)
     pl.semaphore_wait(barrier, 9)
 
     own = g * 4
@@ -96,72 +100,82 @@
     def block(yy, cc):
         return (yy * 2 + cc) * 4
 
-    def adapters(kind, src, gathered):
-        base = kind * 16
-        below, above, across = block(off(y, 3), core), block(off(y, 1), core), block(off(y, 2), core)
-
-        def cp(k, source, unit, count, to):
-            return remote(source, gathered.at[pl.ds(unit, count)], y_send.at[base + k], y_recv.at[base + k], to)
-
-        def here(unit, count):
-            return gathered.at[pl.ds(unit, count)]
-
-        first = [
-            cp(0, src.at[pl.ds(0, 2)], own, 2, y_up),
-            cp(1, src.at[pl.ds(2, 2)], own + 2, 2, y_down),
-            cp(2, src.at[pl.ds(2, 2)], own + 2, 2, y_up),
-            cp(3, src.at[pl.ds(0, 2)], own, 2, y_down),
-            cp(4, src, own, 4, sibling),
-        ]
-        second = [
-            cp(5, here(below, 2), below, 2, y_up),
-            cp(6, here(above + 2, 2), above + 2, 2, y_down),
-            cp(7, here(below, 4), below, 4, sibling),
-            cp(8, here(above, 4), above, 4, sibling),
-        ]
-        third = [
-            cp(9, here(across, 2), across, 2, sibling),
-            cp(10, here(across + 2, 2), across + 2, 2, sibling),
-        ]
-        return first, second, third
-
-    dn1, dn2, dn3 = adapters(0, down, gdn)
-    up1, up2, up3 = adapters(1, up_t, gup)
+    below, above, across = block(off(y, 3), core), block(off(y, 1), core), block(off(y, 2), core)
+
+    class Gather:
+        def __init__(self, kind, src, gathered):
+            self.kind, self.src, self.all = kind, src, gathered
+
+        def send(self, source, unit, count, sem, to):
+            remote(source, self.all.at[pl.ds(unit, count)], y_send.at[self.kind], y_recv.at[self.kind, sem], to).start()
+
+        def own(self, k):
+            self.send(self.src.at[pl.ds(k, 1)], own + k, 1, min(k, 2), y_up)
+            m = (k + 2) % 4
+            self.send(self.src.at[pl.ds(m, 1)], own + m, 1, 4 + min(k, 2), y_down)
+
+        def pass_on(self, k):
+            self.wait(k, 1)
+            self.send(self.all.at[pl.ds(below + k, 1)], below + k, 1, 3, y_up)
+            self.wait(4 + k, 1)
+            self.send(self.all.at[pl.ds(above + 2 + k, 1)], above + 2 + k, 1, 7, y_down)
+
+        def share_own(self):
+            self.send(self.src, own, 4, 8, sibling)
+
+        def share_near(self):
+            self.wait(2, 2)
+            self.wait(6, 2)
+            self.send(self.all.at[pl.ds(below, 4)], below, 4, 9, sibling)
+            self.send(self.all.at[pl.ds(above, 4)], above, 4, 9, sibling)
+
+        def share_far(self):
+            self.wait(3, 2)
+            self.wait(7, 2)
+            self.send(self.all.at[pl.ds(across, 4)], across, 4, 10, sibling)
+
+        def wait(self, sem, units):
+            arrived(self.all.at[pl.ds(0, units)], y_recv.at[self.kind, sem])
+
+        def wait_shared(self):
+            self.wait(8, 4)
+            self.wait(9, 8)
+            self.wait(10, 4)
+
+        def wait_sent(self):
+            arrived(self.all.at[pl.ds(0, 28)], y_send.at[self.kind])
+
+    dn = Gather(0, down, gdn)
+    up = Gather(1, up_t, gup)
 
     def start(copies):
         for c in copies:
             c.start()
 
-    def got(copies):
-        for c in copies:
-            c.wait_recv()
-
-    start(dn1)
+    dn.own(0)
+    dn.own(1)
     own_dn = pltpu.make_async_copy(down, gdn.at[pl.ds(own, 4)], own_sem.at[0])
     own_up = pltpu.make_async_copy(up_t, gup.at[pl.ds(own, 4)], own_sem.at[1])
-    own_dn.start()
-    own_up.start()
-    w_start(0, 0)
-    w_start(1, 1)
 
     vup_copy.wait()
 
-    @pl.loop(0, 4)
-    def _(c):
-        slot = lax.rem(c, 2)
+    def heads_rows(c):
+        slot = c % 2
         lat_wait(slot)
         for k in range(4):
             for m in range(4):
-                wide[k, pl.ds(m * 512, 512), :] = p[slot, k, m].astype(F32)
-
-        @pl.when(c < 2)
-        def _():
+                wide[k, pl.ds(m * 512, 512), :] = p[slot + 1, k, m].astype(F32)
+
+        if c < 2:
             lat_start(c + 2, slot)
-
         for h in range(8):
             xh = jnp.concatenate([wide[k, pl.ds(h, 256, stride=8), :] for k in range(4)], axis=1).astype(BF16)
-            heads[pl.ds(pl.multiple_of(c * 256, 256), 256), pl.ds(h * 128, 128)] = jnp.dot(
+            heads[pl.ds(c * 256, 256), pl.ds(h * 128, 128)] = jnp.dot(
                 xh, vup[h], preferred_element_type=F32).astype(BF16)
+
+    heads_rows(0)
+    heads_rows(1)
+    w_start(1, 1)
 
     coord = (x, z)
     ring = (x_at, z_at)
@@ -177,37 +191,40 @@
             me, to = coord[dim], ring[dim]
             plus, opp, minus = off(me, 1), off(me, 2), off(me, 3)
             what = {0: ((opp, 0), (opp, 1)), 1: ((plus, 1), (minus, 0)), 2: ((plus, 0), (minus, 1))}[kind]
-            land = (s1r.at[n1], s2r.at[n5], s3r.at[n5])[kind]
+            land = (s1r.at[n1], s23r.at[n5, 0], s23r.at[n5, 1])[kind]
+            sem = s1_recv.at[n1] if kind == 0 else s23_recv.at[n5]
             for way in range(2):
                 dest, half = what[way]
                 copies.append(remote(
                     piece(slot, dim, dest, half), land.at[dim, way],
-                    s_send.at[kind, c, dim, way], s_recv.at[kind, c, dim, way], to[1] if way == 0 else to[3]))
+                    s_send.at[slot], sem, to[1] if way == 0 else to[3]))
         return copies
 
     def t_copies(c, kind):
-        slot = lax.rem(c, R_SLOTS)
+        slot, n3, n5 = lax.rem(c, R_SLOTS), lax.rem(c, S1_SLOTS), lax.rem(c, S23_SLOTS)
         copies = []
         for dim in range(2):
             me, to = coord[1 - dim], ring[1 - dim]
             plus, opp, minus = off(me, 1), off(me, 2), off(me, 3)
             what = {0: ((opp, 0), (opp, 1)), 1: ((plus, 1), (minus, 0)), 2: ((plus, 0), (minus, 1))}[kind]
-            land = (t1r, t2r, t3r)[kind]
+            land = (t1r.at[n3], t23r.at[n5, 0], t23r.at[n5, 1])[kind]
+            sem = t1_recv.at[n3] if kind == 0 else t23_recv.at[n5]
             for way in range(2):
                 dest, half = what[way]
                 copies.append(remote(
-                    r.at[slot, dim, dest, pl.ds(half * 128, 128), :], land.at[c, dim, way],
-                    t_send.at[kind, c, dim, way], t_recv.at[kind, c, dim, way], to[1] if way == 0 else to[3]))
+                    r.at[slot, dim, dest, pl.ds(half * 128, 128), :], land.at[dim, way],
+                    t_send.at[slot], sem, to[1] if way == 0 else to[3]))
         return copies
+
+    def s_sent(slot):
+        arrived(p.at[slot, pl.ds(0, 3)], s_send.at[slot])
 
     def produce(c):
         slot = lax.rem(c, P_SLOTS)
 
         @pl.when(c >= P_SLOTS)
         def _():
-            for kind in range(3):
-                for cp in s_copies(c - P_SLOTS, kind):
-                    cp.wait_send()
+            s_sent(slot)
 
         @pl.when(c < 6)
         def _():
@@ -235,8 +252,7 @@
 
         @pl.when(c == 6)
         def _():
-            tail = w.at[1, :, :, pl.ds(0, 128)]
-            pltpu.make_async_copy(tail, tail, w_sem.at[1]).wait()
+            arrived(w.at[1, :, :, pl.ds(0, 128)], w_sem.at[1])
             lane = lax.broadcasted_iota(jnp.int32, (512, 128), 1)
 
             @pl.loop(0, 8)
@@ -252,7 +268,7 @@
 
     def pass_on(c):
         slot, n1 = lax.rem(c, P_SLOTS), lax.rem(c, S1_SLOTS)
-        got(s_copies(c, 0))
+        arrived(s1r.at[n1], s1_recv.at[n1])
         for dim in range(2):
             for way in range(2):
                 dest = off(coord[dim], 1 if way == 0 else 3)
@@ -262,38 +278,34 @@
 
     def reduce_first(c):
         slot, n5, rs = lax.rem(c, P_SLOTS), lax.rem(c, S23_SLOTS), lax.rem(c, R_SLOTS)
-        got(s_copies(c, 1))
-        got(s_copies(c, 2))
+        arrived(s23r.at[n5], s23_recv.at[n5])
         for dim in range(2):
             for half in range(2):
                 mine = piece(slot, dim, coord[dim], half)[...].astype(F32)
-                total = mine + s3r[n5, dim, half].astype(F32) + s2r[n5, dim, 1 - half].astype(F32)
+                total = mine + s23r[n5, 1, dim, half].astype(F32) + s23r[n5, 0, dim, 1 - half].astype(F32)
                 r[rs, dim, :, pl.ds(half * 128, 128), :] = total.astype(BF16)
         start(t_copies(c, 0))
         start(t_copies(c, 1))
 
     def pass_on_second(c):
-        rs = lax.rem(c, R_SLOTS)
-        got(t_copies(c, 0))
+        rs, n3 = lax.rem(c, R_SLOTS), lax.rem(c, S1_SLOTS)
+        arrived(t1r.at[n3], t1_recv.at[n3])
         for dim in range(2):
             for way in range(2):
                 dest = off(coord[1 - dim], 1 if way == 0 else 3)
                 ref = r.at[rs, dim, dest, pl.ds(way * 128, 128), :]
-                ref[...] = (ref[...].astype(F32) + t1r[c, dim, way].astype(F32)).astype(BF16)
+                ref[...] = (ref[...].astype(F32) + t1r[n3, dim, way].astype(F32)).astype(BF16)
         start(t_copies(c, 2))
 
     def reduce_second(c):
-        rs = lax.rem(c, R_SLOTS)
-        got(t_copies(c, 1))
-        got(t_copies(c, 2))
+        rs, n5 = lax.rem(c, R_SLOTS), lax.rem(c, S23_SLOTS)
+        arrived(t23r.at[n5], t23_recv.at[n5])
         for dim in range(2):
             for half in range(2):
                 mine = r[rs, dim, coord[1 - dim], pl.ds(half * 128, 128), :].astype(F32)
                 f[c, pl.ds(dim * 256 + half * 128, 128), :] = (
-                    mine + t3r[c, dim, half].astype(F32) + t2r[c, dim, 1 - half].astype(F32))
-        for kind in range(3):
-            for cp in t_copies(c, kind):
-                cp.wait_send()
+                    mine + t23r[n5, 1, dim, half].astype(F32) + t23r[n5, 0, dim, 1 - half].astype(F32))
+        arrived(r.at[rs, :, pl.ds(0, 3)], t_send.at[rs])
 
     def l_copies(phase):
         copies = []
@@ -314,26 +326,24 @@
                 else:
                     src = dst = lowf.at[mine]
                     dev = to[k]
-                copies.append(remote(src, dst, l_send.at[phase, dim, k - 1], l_recv.at[phase, dim, k - 1], dev))
+                copies.append(remote(src, dst, l_send.at[phase], l_recv.at[phase], dev))
         return copies
 
     def low_images():
         own_dn.wait()
-        got(dn1[4:])
-        got(dn2[2:])
-        got(dn3)
+        dn.wait_shared()
 
         @pl.loop(0, 8)
         def _(q):
             rows = pl.ds(pl.multiple_of((q // 2) * 256, 256), 256)
-            chosen = gdn[ids[q // 2, lax.rem(q, 2)]]
+            chosen = gdn[ids[lax.rem(q, 2), q // 2]]
             low[q] = lax.dot_general(
                 heads[rows, :], chosen, (((1,), (1,)), ((), ())), preferred_element_type=F32).astype(BF16)
 
         start(l_copies(0))
 
     def low_second():
-        got(l_copies(0))
+        arrived(l1r, l_recv.at[0])
         for dim in range(2):
             total = low[dim * 4 + coord[dim]].astype(F32)
             for k in range(3):
@@ -342,7 +352,7 @@
         start(l_copies(1))
 
     def low_third():
-        got(l_copies(1))
+        arrived(l2r, l_recv.at[1])
         for dim in range(2):
             part = pl.ds(pl.multiple_of(coord[1 - dim] * 64, 64), 64)
             total = mid[dim, part, :].astype(F32)
@@ -352,7 +362,7 @@
         start(l_copies(2))
 
     def low_fourth():
-        got(l_copies(2))
+        arrived(l2r, l_recv.at[2])
         start(l_copies(3))
 
     @pl.loop(0, CHUNKS + LAG)
@@ -377,16 +387,39 @@
         def _():
             reduce_second(i - 4)
 
+        @pl.when(i == 0)
+        def _():
+            dn.own(2)
+            own_dn.start()
+            heads_rows(2)
+            heads_rows(3)
+            dn.share_own()
+
+        @pl.when(i == 1)
+        def _():
+            dn.own(3)
+            own_up.start()
+
+        @pl.when(i == 3)
+        def _():
+            dn.pass_on(0)
+
         @pl.when(i == 4)
         def _():
-            got(dn1[:4])
-            start(dn2)
+            dn.pass_on(1)
+
+        @pl.when(i == 5)
+        def _():
+            dn.share_near()
 
         @pl.when(i == 6)
         def _():
-            got(dn2[:2])
-            start(dn3)
-            start(up1)
+            up.own(0)
+            up.own(1)
+            dn.share_far()
+            up.own(2)
+            up.own(3)
+            up.share_own()
 
         @pl.when(i == 7)
         def _():
@@ -399,24 +432,20 @@
         @pl.when(i == 9)
         def _():
             low_third()
-            got(up1[:4])
-            start(up2)
+            up.pass_on(0)
+            up.pass_on(1)
 
         @pl.when(i == 10)
         def _():
             low_fourth()
 
     for c in range(CHUNKS - P_SLOTS, CHUNKS):
-        for kind in range(3):
-            for cp in s_copies(c, kind):
-                cp.wait_send()
-    got(l_copies(3))
-    got(up2[:2])
-    start(up3)
+        s_sent(c % P_SLOTS)
+    up.share_near()
+    arrived(lowf.at[pl.ds(0, 6)], l_recv.at[3])
+    up.share_far()
     own_up.wait()
-    got(up1[4:])
-    got(up2[2:])
-    got(up3)
+    up.wait_shared()
 
     lane = lax.broadcasted_iota(jnp.int32, (256, 128), 1)
     for b in range(4):
@@ -425,7 +454,7 @@
         lifted = None
         for k in range(2):
             li = lax.dot_general(
-                lowf[b * 2 + k], gup[ids[b, k]], (((1,), (1,)), ((), ())),
+                lowf[b * 2 + k], gup[ids[k, b]], (((1,), (1,)), ((), ())),
                 preferred_element_type=F32).astype(BF16).astype(F32)
             weight = jnp.broadcast_to(mix[k:k + 1, b * 256:(b + 1) * 256], (128, 256)).T
             li = [li[:, :128] * weight, li[:, 128:256] * weight, li[:, 256:384] * weight, li[:, 384:] * weight[:, :64]]
@@ -437,8 +466,8 @@
 
         def write(tiles):
             for t in range(3):
-                out[rows, pl.ds(t * 128, 128)] = (tiles[t] + lifted[t]).astype(BF16)
-            out[rows, pl.ds(384, 64)] = (tiles[3][:, :64] + lifted[3]).astype(BF16)
+                staged[rows, pl.ds(t * 128, 128)] = (tiles[t] + lifted[t]).astype(BF16)
+            staged[rows, pl.ds(384, 64)] = (tiles[3][:, :64] + lifted[3]).astype(BF16)
 
         @pl.when(lax.rem(z, 2) == 0)
         def _():
@@ -454,9 +483,13 @@
                 turned[2],
             ])
 
-    for copies in (dn1, dn2, dn3, up1, up2, up3, l_copies(0), l_copies(1), l_copies(2), l_copies(3)):
-        for cp in copies:
-            cp.wait_send()
+        pltpu.make_async_copy(staged.at[rows], out.at[rows], out_sem).start()
+
+    arrived(staged, out_sem)
+    dn.wait_sent()
+    up.wait_sent()
+    for phase, ref in enumerate((low.at[pl.ds(0, 6)], l2r, l2r, low.at[pl.ds(0, 6)])):
+        arrived(ref, l_send.at[phase])
 
 
 def local(latent, value_up, out_proj, adapter_down, adapter_up, pair_ids, mix_weights):
@@ -472,12 +505,10 @@
         pltpu.VMEM((2, 8, 1024, 256), BF16),
         pltpu.VMEM((P_SLOTS, 4, 4, 512, 128), BF16),
         pltpu.VMEM((S1_SLOTS, 2, 2, 4, 128, 128), BF16),
-        pltpu.VMEM((S23_SLOTS, 2, 2, 4, 128, 128), BF16),
-        pltpu.VMEM((S23_SLOTS, 2, 2, 4, 128, 128), BF16),
+        pltpu.VMEM((S23_SLOTS, 2, 2, 2, 4, 128, 128), BF16),
         pltpu.VMEM((R_SLOTS, 2, 4, 256, 128), BF16),
-        pltpu.VMEM((CHUNKS, 2, 2, 128, 128), BF16),
-        pltpu.VMEM((CHUNKS, 2, 2, 128, 128), BF16),
-        pltpu.VMEM((CHUNKS, 2, 2, 128, 128), BF16),
+        pltpu.VMEM((S1_SLOTS, 2, 2, 128, 128), BF16),
+        pltpu.VMEM((S23_SLOTS, 2, 2, 2, 128, 128), BF16),
         pltpu.VMEM((CHUNKS, 512, 128), F32),
         pltpu.VMEM((32, 256, 1024), BF16),
         pltpu.VMEM((32, 448, 256), BF16),
@@ -486,24 +517,24 @@
         pltpu.VMEM((2, 256, 256), BF16),
         pltpu.VMEM((2, 3, 64, 256), BF16),
         pltpu.VMEM((8, 256, 256), BF16),
-        dma((2,)), dma, dma((2,)), dma((2,)),
-        dma((3, CHUNKS, 2, 2)), dma((3, CHUNKS, 2, 2)),
-        dma((3, CHUNKS, 2, 2)), dma((3, CHUNKS, 2, 2)),
-        dma((32,)), dma((32,)),
-        dma((4, 2, 3)), dma((4, 2, 3)),
+        pltpu.VMEM((rows, 448), BF16),
+        dma((2,)), dma, dma((2,)), dma((2,)), dma,
+        dma((P_SLOTS,)), dma((S1_SLOTS,)), dma((S23_SLOTS,)),
+        dma((R_SLOTS,)), dma((S1_SLOTS,)), dma((S23_SLOTS,)),
+        dma((2,)), dma((2, 11)), dma((4,)), dma((4,)),
     ]
     return pl.pallas_call(
         kernel,
         out_shape=jax.ShapeDtypeStruct((rows, adapter_up.shape[2]), BF16),
         in_specs=[any_, any_, any_, any_, any_, smem, vmem],
-        out_specs=vmem,
+        out_specs=any_,
         scratch_shapes=scratch,
         compiler_params=pltpu.CompilerParams(
             collective_id=1, has_side_effects=True, vmem_limit_bytes=64 << 20),
         name="project",
     )(
         latent.reshape(rows * 8, 512), value_up, out_proj, adapter_down,
-        jnp.swapaxes(adapter_up, 1, 2), pair_ids, mix_weights,
+        jnp.swapaxes(adapter_up, 1, 2), pair_ids.T, mix_weights,
     )
 
 

time: 129 us -> 120 us (0.930)
  Pallas kernels: 125 us -> 117 us
  local copies, waits for them, and re-layouts: 3.55 us -> 2.22 us
    pallas_call x1, Pallas kernels: 125 us -> 117 us  [local(): pl.pallas_call(kernel, out_shape=jax.ShapeDtypeStruct((rows, adapter_up.s...]
    unnamed x1 -> x0, local copies, waits for them, and re-layouts: 1.34 us -> none
where the time goes in v2:
time: 120 us
  Pallas kernels  117 us (98%)
  local copies, waits for them, and re-layouts  2.22 us (2%)
    pallas_call x1, Pallas kernels, local(): pl.pallas_call(kernel, out_shape=jax.ShapeDtypeStruct((rows, adapter_up.s...  117 us

profile of v2, /device:TPU:1, one launch (start us, length us, event | category | flops | bytes accessed | tf_op | source)
XLA Modules:
  0.0 119.6 jit_solution(10787542528109244589)
XLA Ops:
  0.0 117.4 %project.1 = bf16[1024,448]{1,0:T(8,128)(2,1)} custom-call(bf16[8192,512]{1,0:T(8,128)(2,1)} %bitcast.3, bf16[8,512,128]{2,1,0:T(8,128)(2,1)} %value_up.1, bf16[1024,7168]{1,0:T(8,128)(2,1)} %out_proj.1, bf16[4,256,1024]{2,1,0:T(8,128)(2,1)} %down.1, bf16[4,448,256]{2,1,0:T(8,128)(2,1)} %bitcast.4, s32[2,4]{1,0:T(2,128)} %bitcast.5, f32[2,1024]{1,0:T(2,128)} %mix.1), custom_call_target="tpu_custom_call" | custom-call | tf_op jit(solution)/shard_map/project/pallas_call | solution.py:526
  117.4 2.2 %copy.8 = bf16[1024,448]{0,1:T(8,128)(2,1)} copy(bf16[1024,448]{1,0:T(8,128)(2,1)} %project.1) | data formatting | bytes 1835008 | tf_op jit(solution)/shard_map/project/pallas_call | solution.py:526

commit v3 on v2

--- a/solution.py
+++ b/solution.py
@@ -10,12 +10,12 @@
 MESH = pl.DeviceIdType.MESH
 F32 = jnp.float32
 BF16 = jnp.bfloat16
-CHUNKS = 7
-LAG = 4
+CHUNKS = 14
+LAG = 2
 P_SLOTS = 3
-S1_SLOTS = 3
-S23_SLOTS = 5
-R_SLOTS = 3
+S1_SLOTS = 5
+S23_SLOTS = 8
+R_SLOTS = 5
 
 
 def roll64(x):
@@ -24,7 +24,7 @@
 
 def kernel(
     latent, value_up, out_proj, down, up_t, ids, mix, out,
-    wide, vup, heads, w, p, s1r, s23r, r, t1r, t23r, f,
+    lat, wide, vup, heads, w, p, s1r, s23r, r, t1r, t23r, f,
     gdn, gup, low, l1r, mid, l2r, lowf, staged,
     lat_sem, vup_sem, w_sem, own_sem, out_sem,
     s_send, s1_recv, s23_recv, t_send, t1_recv, t23_recv, y_send, y_recv, l_send, l_recv,
@@ -62,13 +62,9 @@
 
     def lat_start(c, slot):
         for k in range(4):
-            for m in range(4):
-                pltpu.make_async_copy(
-                    latent.at[pl.ds(pl.multiple_of(c * 2048 + m * 512, 512), 512), pl.ds(k * 128, 128)],
-                    p.at[slot + 1, k, m], lat_sem.at[slot]).start()
-
-    def lat_wait(slot):
-        arrived(p.at[slot + 1], lat_sem.at[slot])
+            pltpu.make_async_copy(
+                latent.at[pl.ds(pl.multiple_of(c * 2048, 2048), 2048), pl.ds(k * 128, 128)],
+                lat.at[slot, k], lat_sem.at[slot]).start()
 
     def w_start(t, slot):
         @pl.loop(0, 8)
@@ -160,32 +156,34 @@
     vup_copy.wait()
 
     def heads_rows(c):
-        slot = c % 2
-        lat_wait(slot)
+        slot = lax.rem(c, 2)
+        arrived(lat.at[slot], lat_sem.at[slot])
         for k in range(4):
-            for m in range(4):
-                wide[k, pl.ds(m * 512, 512), :] = p[slot + 1, k, m].astype(F32)
-
-        if c < 2:
+            wide[k] = lat[slot, k].astype(F32)
+
+        @pl.when(c < 2)
+        def _():
             lat_start(c + 2, slot)
+
         for h in range(8):
             xh = jnp.concatenate([wide[k, pl.ds(h, 256, stride=8), :] for k in range(4)], axis=1).astype(BF16)
-            heads[pl.ds(c * 256, 256), pl.ds(h * 128, 128)] = jnp.dot(
+            heads[pl.ds(pl.multiple_of(c * 256, 256), 256), pl.ds(h * 128, 128)] = jnp.dot(
                 xh, vup[h], preferred_element_type=F32).astype(BF16)
 
-    heads_rows(0)
-    heads_rows(1)
+    heads_rows(jnp.int32(0))
+    heads_rows(jnp.int32(1))
     w_start(1, 1)
 
     coord = (x, z)
     ring = (x_at, z_at)
 
-    def piece(slot, dim, dest, half):
-        rows = pl.ds(dim * 256 + half * 128, 128)
+    def piece(c, dim, dest, half):
+        slot = lax.rem(c // 2, P_SLOTS)
+        rows = pl.ds(pl.multiple_of(lax.rem(c, 2) * 256 + dim * 128 + half * 64, 64), 64)
         return p.at[slot, dest, :, rows, :] if dim == 0 else p.at[slot, :, dest, rows, :]
 
     def s_copies(c, kind):
-        slot, n1, n5 = lax.rem(c, P_SLOTS), lax.rem(c, S1_SLOTS), lax.rem(c, S23_SLOTS)
+        slot, n1, n5 = lax.rem(c // 2, P_SLOTS), lax.rem(c, S1_SLOTS), lax.rem(c, S23_SLOTS)
         copies = []
         for dim in range(2):
             me, to = coord[dim], ring[dim]
@@ -196,7 +194,7 @@
             for way in range(2):
                 dest, half = what[way]
                 copies.append(remote(
-                    piece(slot, dim, dest, half), land.at[dim, way],
+                    piece(c, dim, dest, half), land.at[dim, way],
                     s_send.at[slot], sem, to[1] if way == 0 else to[3]))
         return copies
 
@@ -212,7 +210,7 @@
             for way in range(2):
                 dest, half = what[way]
                 copies.append(remote(
-                    r.at[slot, dim, dest, pl.ds(half * 128, 128), :], land.at[dim, way],
+                    r.at[slot, dim, dest, pl.ds(half * 64, 64), :], land.at[dim, way],
                     t_send.at[slot], sem, to[1] if way == 0 else to[3]))
         return copies
 
@@ -263,27 +261,24 @@
                 p[slot, q // 2, lax.rem(q, 2) * 2] = jnp.where(lane < 64, top, roll64(bottom)).astype(BF16)
                 p[slot, q // 2, lax.rem(q, 2) * 2 + 1] = jnp.where(lane < 64, roll64(top), bottom).astype(BF16)
 
-        start(s_copies(c, 0))
-        start(s_copies(c, 1))
-
     def pass_on(c):
-        slot, n1 = lax.rem(c, P_SLOTS), lax.rem(c, S1_SLOTS)
+        n1 = lax.rem(c, S1_SLOTS)
         arrived(s1r.at[n1], s1_recv.at[n1])
         for dim in range(2):
             for way in range(2):
                 dest = off(coord[dim], 1 if way == 0 else 3)
-                ref = piece(slot, dim, dest, way)
+                ref = piece(c, dim, dest, way)
                 ref[...] = (ref[...].astype(F32) + s1r[n1, dim, way].astype(F32)).astype(BF16)
         start(s_copies(c, 2))
 
     def reduce_first(c):
-        slot, n5, rs = lax.rem(c, P_SLOTS), lax.rem(c, S23_SLOTS), lax.rem(c, R_SLOTS)
+        n5, rs = lax.rem(c, S23_SLOTS), lax.rem(c, R_SLOTS)
         arrived(s23r.at[n5], s23_recv.at[n5])
         for dim in range(2):
             for half in range(2):
-                mine = piece(slot, dim, coord[dim], half)[...].astype(F32)
+                mine = piece(c, dim, coord[dim], half)[...].astype(F32)
                 total = mine + s23r[n5, 1, dim, half].astype(F32) + s23r[n5, 0, dim, 1 - half].astype(F32)
-                r[rs, dim, :, pl.ds(half * 128, 128), :] = total.astype(BF16)
+                r[rs, dim, :, pl.ds(half * 64, 64), :] = total.astype(BF16)
         start(t_copies(c, 0))
         start(t_copies(c, 1))
 
@@ -293,7 +288,7 @@
         for dim in range(2):
             for way in range(2):
                 dest = off(coord[1 - dim], 1 if way == 0 else 3)
-                ref = r.at[rs, dim, dest, pl.ds(way * 128, 128), :]
+                ref = r.at[rs, dim, dest, pl.ds(way * 64, 64), :]
                 ref[...] = (ref[...].astype(F32) + t1r[n3, dim, way].astype(F32)).astype(BF16)
         start(t_copies(c, 2))
 
@@ -302,8 +297,8 @@
         arrived(t23r.at[n5], t23_recv.at[n5])
         for dim in range(2):
             for half in range(2):
-                mine = r[rs, dim, coord[1 - dim], pl.ds(half * 128, 128), :].astype(F32)
-                f[c, pl.ds(dim * 256 + half * 128, 128), :] = (
+                mine = r[rs, dim, coord[1 - dim], pl.ds(half * 64, 64), :].astype(F32)
+                f[c, pl.ds(dim * 128 + half * 64, 64), :] = (
                     mine + t23r[n5, 1, dim, half].astype(F32) + t23r[n5, 0, dim, 1 - half].astype(F32))
         arrived(r.at[rs, :, pl.ds(0, 3)], t_send.at[rs])
 
@@ -365,126 +360,134 @@
         arrived(l2r, l_recv.at[2])
         start(l_copies(3))
 
-    @pl.loop(0, CHUNKS + LAG)
+    @pl.loop(0, CHUNKS + 4 * LAG)
     def _(i):
+        @pl.when((i < CHUNKS) & (lax.rem(i, 2) == 0))
+        def _():
+            produce(i // 2)
+
         @pl.when(i < CHUNKS)
         def _():
-            produce(i)
-
-        @pl.when((i >= 1) & (i < CHUNKS + 1))
-        def _():
-            pass_on(i - 1)
-
-        @pl.when((i >= 2) & (i < CHUNKS + 2))
-        def _():
-            reduce_first(i - 2)
-
-        @pl.when((i >= 3) & (i < CHUNKS + 3))
-        def _():
-            pass_on_second(i - 3)
-
-        @pl.when(i >= 4)
-        def _():
-            reduce_second(i - 4)
+            start(s_copies(i, 0))
+            start(s_copies(i, 1))
+
+        for stage, work in enumerate((pass_on, reduce_first, pass_on_second, reduce_second)):
+            behind = (stage + 1) * LAG
+            pl.when((i >= behind) & (i < CHUNKS + behind))(functools.partial(work, i - behind))
+
+        @pl.when(i < 2)
+        def _():
+            heads_rows(i + 2)
 
         @pl.when(i == 0)
         def _():
+            own_dn.start()
+
+        @pl.when(i == 1)
+        def _():
             dn.own(2)
-            own_dn.start()
-            heads_rows(2)
-            heads_rows(3)
             dn.share_own()
-
-        @pl.when(i == 1)
+            own_up.start()
+
+        @pl.when(i == 2)
         def _():
             dn.own(3)
-            own_up.start()
-
-        @pl.when(i == 3)
+
+        @pl.when(i == 5)
         def _():
             dn.pass_on(0)
 
-        @pl.when(i == 4)
+        @pl.when(i == 7)
         def _():
             dn.pass_on(1)
 
-        @pl.when(i == 5)
+        @pl.when(i == 9)
         def _():
             dn.share_near()
 
-        @pl.when(i == 6)
+        @pl.when(i == 10)
         def _():
             up.own(0)
             up.own(1)
+
+        @pl.when(i == 12)
+        def _():
             dn.share_far()
             up.own(2)
             up.own(3)
             up.share_own()
 
-        @pl.when(i == 7)
+        @pl.when(i == 13)
         def _():
             low_images()
 
-        @pl.when(i == 8)
+        @pl.when(i == 15)
         def _():
             low_second()
-
-        @pl.when(i == 9)
+            up.pass_on(0)
+
+        @pl.when(i == 17)
         def _():
             low_third()
-            up.pass_on(0)
             up.pass_on(1)
 
-        @pl.when(i == 10)
+        @pl.when(i == 19)
         def _():
             low_fourth()
-
-    for c in range(CHUNKS - P_SLOTS, CHUNKS):
-        s_sent(c % P_SLOTS)
-    up.share_near()
-    arrived(lowf.at[pl.ds(0, 6)], l_recv.at[3])
+            up.share_near()
+
     up.share_far()
     own_up.wait()
-    up.wait_shared()
 
     lane = lax.broadcasted_iota(jnp.int32, (256, 128), 1)
     for b in range(4):
-        half, at_row = b // 2, (b % 2) * 256
-        rows = pl.ds(b * 256, 256)
-        lifted = None
-        for k in range(2):
-            li = lax.dot_general(
-                lowf[b * 2 + k], gup[ids[k, b]], (((1,), (1,)), ((), ())),
-                preferred_element_type=F32).astype(BF16).astype(F32)
-            weight = jnp.broadcast_to(mix[k:k + 1, b * 256:(b + 1) * 256], (128, 256)).T
-            li = [li[:, :128] * weight, li[:, 128:256] * weight, li[:, 256:384] * weight, li[:, 384:] * weight[:, :64]]
-            lifted = li if lifted is None else [u + v for u, v in zip(lifted, li)]
-        main = [f[2 * t + half, pl.ds(at_row, 256), :] for t in range(3)]
-        tail = f[6, pl.ds(at_row, 256), :]
-        if half == 1:
+        main = [f[4 * t + b] for t in range(3)]
+        tail = f[12 + b % 2]
+        if b >= 2:
             tail = roll64(tail)
 
-        def write(tiles):
-            for t in range(3):
-                staged[rows, pl.ds(t * 128, 128)] = (tiles[t] + lifted[t]).astype(BF16)
-            staged[rows, pl.ds(384, 64)] = (tiles[3][:, :64] + lifted[3]).astype(BF16)
+        def keep(tiles):
+            for t in range(4):
+                wide[b, pl.ds(t * 256, 256), :] = tiles[t]
 
         @pl.when(lax.rem(z, 2) == 0)
         def _():
-            write(main + [tail])
+            keep(main + [tail])
 
         @pl.when(lax.rem(z, 2) == 1)
         def _():
             turned = [roll64(m) for m in main]
-            write([
+            keep([
                 jnp.where(lane < 64, tail, turned[0]),
                 jnp.where(lane < 64, turned[0], turned[1]),
                 jnp.where(lane < 64, turned[1], turned[2]),
                 turned[2],
             ])
 
+        for k in range(2):
+            wide[b, pl.ds(1024 + k * 256, 256), :] = jnp.broadcast_to(mix[k:k + 1, b * 256:(b + 1) * 256], (128, 256)).T
+
+    arrived(lowf.at[pl.ds(0, 6)], l_recv.at[3])
+    up.wait_shared()
+
+    for b in range(4):
+        rows = pl.ds(b * 256, 256)
+        first, second = [
+            lax.dot_general(
+                lowf[b * 2 + k], gup[ids[k, b]], (((1,), (1,)), ((), ())),
+                preferred_element_type=F32).astype(BF16).astype(F32)
+            for k in range(2)
+        ]
+        w0, w1 = wide[b, pl.ds(1024, 256), :], wide[b, pl.ds(1280, 256), :]
+        for t in range(4):
+            n = 128 if t < 3 else 64
+            cols = slice(t * 128, t * 128 + n)
+            mixed = wide[b, pl.ds(t * 256, 256), :][:, :n] + (w0[:, :n] * first[:, cols] + w1[:, :n] * second[:, cols])
+            staged[rows, pl.ds(t * 128, n)] = mixed.astype(BF16)
         pltpu.make_async_copy(staged.at[rows], out.at[rows], out_sem).start()
 
+    for slot in range(P_SLOTS):
+        s_sent(slot)
     arrived(staged, out_sem)
     dn.wait_sent()
     up.wait_sent()
@@ -499,17 +502,18 @@
     smem = pl.BlockSpec(memory_space=pltpu.SMEM)
     dma = pltpu.SemaphoreType.DMA
     scratch = [
+        pltpu.VMEM((2, 4, 2048, 128), BF16),
         pltpu.VMEM((4, 2048, 128), F32),
         pltpu.VMEM((8, 512, 128), BF16),
         pltpu.VMEM((rows, 1024), BF16),
         pltpu.VMEM((2, 8, 1024, 256), BF16),
         pltpu.VMEM((P_SLOTS, 4, 4, 512, 128), BF16),
-        pltpu.VMEM((S1_SLOTS, 2, 2, 4, 128, 128), BF16),
-        pltpu.VMEM((S23_SLOTS, 2, 2, 2, 4, 128, 128), BF16),
-        pltpu.VMEM((R_SLOTS, 2, 4, 256, 128), BF16),
-        pltpu.VMEM((S1_SLOTS, 2, 2, 128, 128), BF16),
-        pltpu.VMEM((S23_SLOTS, 2, 2, 2, 128, 128), BF16),
-        pltpu.VMEM((CHUNKS, 512, 128), F32),
+        pltpu.VMEM((S1_SLOTS, 2, 2, 4, 64, 128), BF16),
+        pltpu.VMEM((S23_SLOTS, 2, 2, 2, 4, 64, 128), BF16),
+        pltpu.VMEM((R_SLOTS, 2, 4, 128, 128), BF16),
+        pltpu.VMEM((S1_SLOTS, 2, 2, 64, 128), BF16),
+        pltpu.VMEM((S23_SLOTS, 2, 2, 2, 64, 128), BF16),
+        pltpu.VMEM((CHUNKS, 256, 128), F32),
         pltpu.VMEM((32, 256, 1024), BF16),
         pltpu.VMEM((32, 448, 256), BF16),
         pltpu.VMEM((8, 256, 256), BF16),

time: 120 us -> 116 us (0.967)
  Pallas kernels: 117 us -> 114 us
    pallas_call x1, Pallas kernels: 117 us -> 114 us  [local(): pl.pallas_call(kernel, out_shape=jax.ShapeDtypeStruct((rows, adapter_up.s...]
where the time goes in v3:
time: 116 us
  Pallas kernels  114 us (98%)
  local copies, waits for them, and re-layouts  2.22 us (2%)
    pallas_call x1, Pallas kernels, local(): pl.pallas_call(kernel, out_shape=jax.ShapeDtypeStruct((rows, adapter_up.s...  114 us

profile of v3, /device:TPU:1, one launch (start us, length us, event | category | flops | bytes accessed | tf_op | source)
XLA Modules:
  0.0 116.1 jit_solution(4784049631520902162)
XLA Ops:
  0.0 113.9 %project.1 = bf16[1024,448]{1,0:T(8,128)(2,1)} custom-call(bf16[8192,512]{1,0:T(8,128)(2,1)} %bitcast.3, bf16[8,512,128]{2,1,0:T(8,128)(2,1)} %value_up.1, bf16[1024,7168]{1,0:T(8,128)(2,1)} %out_proj.1, bf16[4,256,1024]{2,1,0:T(8,128)(2,1)} %down.1, bf16[4,448,256]{2,1,0:T(8,128)(2,1)} %bitcast.4, s32[2,4]{1,0:T(2,128)} %bitcast.5, f32[2,1024]{1,0:T(2,128)} %mix.1), custom_call_target="tpu_custom_call" | custom-call | tf_op jit(solution)/shard_map/project/pallas_call | solution.py:530
  113.9 2.2 %copy.8 = bf16[1024,448]{0,1:T(8,128)(2,1)} copy(bf16[1024,448]{1,0:T(8,128)(2,1)} %project.1) | data formatting | bytes 1835008 | tf_op jit(solution)/shard_map/project/pallas_call | solution.py:530

commit v4 on v3

--- a/solution.py
+++ b/solution.py
@@ -397,7 +397,7 @@
         def _():
             dn.pass_on(0)
 
-        @pl.when(i == 7)
+        @pl.when(i == 6)
         def _():
             dn.pass_on(1)
 
@@ -410,28 +410,31 @@
             up.own(0)
             up.own(1)
 
-        @pl.when(i == 12)
-        def _():
-            dn.share_far()
+        @pl.when(i == 11)
+        def _():
             up.own(2)
             up.own(3)
+
+        @pl.when(i == 13)
+        def _():
+            dn.share_far()
             up.share_own()
 
-        @pl.when(i == 13)
+        @pl.when(i == 14)
         def _():
             low_images()
 
-        @pl.when(i == 15)
+        @pl.when(i == 16)
         def _():
             low_second()
             up.pass_on(0)
-
-        @pl.when(i == 17)
+            up.pass_on(1)
+
+        @pl.when(i == 18)
         def _():
             low_third()
-            up.pass_on(1)
-
-        @pl.when(i == 19)
+
+        @pl.when(i == 20)
         def _():
             low_fourth()
             up.share_near()

time: 116 us -> 115 us (level)
  Pallas kernels: 114 us -> 112 us
    pallas_call x1, Pallas kernels: 114 us -> 112 us  [local(): pl.pallas_call(kernel, out_shape=jax.ShapeDtypeStruct((rows, adapter_up.s...]
where the time goes in v4:
time: 115 us
  Pallas kernels  112 us (97%)
  local copies, waits for them, and re-layouts  2.22 us (2%)
    pallas_call x1, Pallas kernels, local(): pl.pallas_call(kernel, out_shape=jax.ShapeDtypeStruct((rows, adapter_up.s...  112 us

profile of v4, /device:TPU:1, one launch (start us, length us, event | category | flops | bytes accessed | tf_op | source)
XLA Modules:
  0.0 114.7 jit_solution(5752921566330024042)
XLA Ops:
  0.0 112.5 %project.1 = bf16[1024,448]{1,0:T(8,128)(2,1)} custom-call(bf16[8192,512]{1,0:T(8,128)(2,1)} %bitcast.3, bf16[8,512,128]{2,1,0:T(8,128)(2,1)} %value_up.1, bf16[1024,7168]{1,0:T(8,128)(2,1)} %out_proj.1, bf16[4,256,1024]{2,1,0:T(8,128)(2,1)} %down.1, bf16[4,448,256]{2,1,0:T(8,128)(2,1)} %bitcast.4, s32[2,4]{1,0:T(2,128)} %bitcast.5, f32[2,1024]{1,0:T(2,128)} %mix.1), custom_call_target="tpu_custom_call" | custom-call | tf_op jit(solution)/shard_map/project/pallas_call | solution.py:533
  112.5 2.2 %copy.8 = bf16[1024,448]{0,1:T(8,128)(2,1)} copy(bf16[1024,448]{1,0:T(8,128)(2,1)} %project.1) | data formatting | bytes 1835008 | tf_op jit(solution)/shard_map/project/pallas_call | solution.py:533
